TPU v7x, 512 devices: a whole 4x8x8 slice. The times are simulated.
512 devices in a mesh: occ: 16 (over y, core), vir: 32 (over x, z).
Axes of the slice: x: 4, y: 8, z: 8, core: 2. Of those that a mesh axis runs over, the one named last changes fastest.
Arguments:
- amplitudes: float32 [2048, 12288], P('occ', 'vir'), may hold values from -6 to 6
- integrals: float32 [12288, 4096], P('vir', 'occ'), may hold values from -0.109375 to 0.109375
- pair_mask: int32 [32, 192], P('occ', 'vir'), may hold values 0 or 1
- tile_mask: int32 [192, 64], P('vir', 'occ'), may hold values 0 or 1
Outputs:
- residual: float32 [2048, 4096], P('occ', 'vir')
Inputs may be any that keep to these rules, and one draw needn't show every extreme that they name: `pair_mask`: 0 marks a tile that is absent and contributes nothing. `tile_mask`: 0 marks a tile that is absent and contributes nothing.
All inputs are finite; a program needn't handle non-finite values. No bound on the sum of `pair_mask` or of `tile_mask` on one device may be relied on, other than what follows from the above.
Results may differ from a plain program's by a relative error of at most 0.00007.
Values sent between devices are 32-bit elements; how exact they have to be, the bound alone decides.
No kernel may reach another device: no remote copies, remote signals or barrier semaphores. Data moves between devices by JAX's collectives and lax.ppermute only.
A program may use at most 64 MiB of HBM per device.

v0:
```python
import jax
import jax.numpy as jnp
from jax import lax
from jax.sharding import Mesh, PartitionSpec as P


def expand(mask, width):
    grown = jnp.repeat(mask.astype(jnp.float32), width, axis=0)
    return jnp.repeat(grown, width, axis=1)


def body(amplitudes, integrals, pair_mask, tile_mask):
    tile_width = amplitudes.shape[1] // pair_mask.shape[1]
    masked_v = integrals * expand(tile_mask, tile_width)
    other_v = lax.ppermute(masked_v, "l", [(0, 1), (1, 0)])
    masked_t = amplitudes * expand(pair_mask, tile_width)
    rows = lax.all_gather(masked_t, "h", axis=0, tiled=True)
    near = lax.all_gather(masked_v, "c", axis=1, tiled=True)
    far = lax.all_gather(other_v, "c", axis=1, tiled=True)
    low = lax.axis_index("l") == 0
    columns = jnp.concatenate([jnp.where(low, near, far), jnp.where(low, far, near)], axis=1)
    partial_sum = jnp.dot(
        rows, columns, precision=lax.Precision.HIGH, preferred_element_type=jnp.float32
    )
    count = lax.axis_size("x")
    parts = lax.all_to_all(partial_sum, "x", 0, 0, tiled=True)
    over_x = parts.reshape(count, -1, parts.shape[1]).sum(0)
    depth = lax.axis_size("z")
    pieces = over_x.reshape(over_x.shape[0], depth, -1).transpose(1, 0, 2)
    pieces = lax.all_to_all(pieces, "z", 0, 0, tiled=True)
    total = pieces.sum(0)
    swap = [(h * count + x, x * count + h) for h in range(count) for x in range(count)]
    return lax.ppermute(total, ("h", "x"), swap)


def solution(mesh):
    fine = Mesh(mesh.devices.reshape(4, 2, 2, 4, 8), ("h", "l", "c", "x", "z"))
    occ, vir = (("h", "l", "c"), ("x", "z"))
    in_specs = (P(occ, vir), P(vir, occ), P(occ, vir), P(vir, occ))
    return jax.shard_map(body, mesh=fine, in_specs=in_specs, out_specs=P(occ, vir), check_vma=False)
```

profile of v0, /device:TPU:4, one launch (start us, length us, event | category | flops | bytes accessed | tf_op | source)
XLA Modules:
  0.0 106.9 jit_solution(17523145308158582603)
XLA Ops:
  0.0 0.7 convert_element_type.7
  0.7 0.1 broadcast_in_dim.14
  0.8 0.1 reshape.21
  0.9 1.2 %copy.21 = f32[384,256]{0,1:T(8,128)S(1)} copy(f32[384,256]{1,0:T(8,128)} %param.5) | data formatting | bytes 786432 | tf_op args[1]
  2.1 3.5 %collective-permute-start = (f32[384,256]{0,1:T(8,128)S(1)}, f32[384,256]{0,1:T(8,128)S(1)}, u32[]{:S(2)}, u32[]{:S(2)}) collective-permute-start(f32[384,256]{0,1:T(8,128)S(1)} %bitcast_multiply_fusion), channel_id=1, source_target_pairs={{0,64},{64,0},{1,65},{65,1},{2,66},{66,2},{3,67},{67,3},{4,68},{68... | collective-permute-start | bytes 1179656 | tf_op jit(solution)/shard_map/ppermute | solution.py:15
  5.6 2.4 %all_gather.10 = f32[384,512]{0,1:T(8,128)S(1)} all-gather(f32[384,256]{0,1:T(8,128)S(1)} %bitcast_multiply_fusion), channel_id=1, replica_groups=mesh['h'=4,'l'=2,'c'=2,'x'=4,'z'=8] {'c'}, dimensions={1}, use_global_device_ids=true | all-gather | bytes 1179648 | tf_op jit(solution)/shard_map/all_gather | solution.py:18
  7.9 0.0 copy-done.1
  8.0 0.1 copy.19
  8.1 0.1 broadcast_in_dim.12
  8.1 0.1 reshape.19
  8.2 0.1 copy.20
  8.4 24.4 %all_gather.9 = f32[512,384]{0,1:T(8,128)S(1)} all-gather(f32[128,384]{0,1:T(8,128)S(1)} %bitcast_multiply_fusion.1), channel_id=1, replica_groups=mesh['h'=4,'l'=2,'c'=2,'x'=4,'z'=8] {'h'}, dimensions={0}, use_global_device_ids=true | all-gather | bytes 983040 | tf_op jit(solution)/shard_map/all_gather | solution.py:17
  32.8 0.0 collective-permute-done
  32.8 2.4 %all_gather.11 = f32[384,512]{0,1:T(8,128)S(1)} all-gather(f32[384,256]{0,1:T(8,128)S(1)} %collective-permute-done), channel_id=1, replica_groups=mesh['h'=4,'l'=2,'c'=2,'x'=4,'z'=8] {'c'}, dimensions={1}, use_global_device_ids=true | all-gather | bytes 1179648 | tf_op jit(solution)/shard_map/all_gather | solution.py:19
  35.2 0.1 broadcast_select_fusion.1
  35.3 2.8 %fusion = f32[512,1024]{1,0:T(8,128)S(1)} fusion(f32[512,384]{0,1:T(8,128)S(1)} %all_gather.9, f32[384,512]{0,1:T(8,128)S(1)} %get-tuple-element.6, f32[384,512]{0,1:T(8,128)S(1)} %get-tuple-element.5), kind=kOutput, calls=%fused_computation | convolution fusion | flops 1208352768 | bytes 4456448 | tf_op jit(solution)/shard_map/dot_general | solution.py:22
  38.1 28.5 %all_to_all.14 = f32[4,128,1024]{2,1,0:T(8,128)S(1)} all-to-all(f32[4,128,1024]{2,1,0:T(8,128)S(1)} %bitcast.13), channel_id=1, replica_groups=mesh['h'=4,'l'=2,'c'=2,'x'=4,'z'=8] {'x'}, dimensions={0} | all-to-all | bytes 4194304 | tf_op jit(solution)/shard_map/all_to_all | solution.py:26
  66.6 0.2 reduce_sum.18
  66.8 0.2 copy.22
  67.0 0.2 copy.23
  67.2 26.5 %all_to_all.15 = f32[8,128,128]{2,1,0:T(8,128)S(1)} all-to-all(f32[8,128,128]{2,1,0:T(8,128)S(1)} %copy.23), channel_id=1, replica_groups=mesh['h'=4,'l'=2,'c'=2,'x'=4,'z'=8] {'z'}, dimensions={0} | all-to-all | bytes 1048576 | tf_op jit(solution)/shard_map/all_to_all | solution.py:30
  93.8 6.3 %collective-permute-start.1 = (f32[128,128]{1,0:T(8,128)S(1)}, f32[128,128]{1,0:T(8,128)S(1)}, u32[]{:S(2)}, u32[]{:S(2)}) collective-permute-start(f32[128,128]{1,0:T(8,128)S(1)} %reduce_sum.19), channel_id=1, source_target_pairs={{0,0},{8,128},{16,256},{24,384},{128,8},{136,136},{144,264},{152,3... | collective-permute-start | bytes 196616 | tf_op jit(solution)/shard_map/ppermute | solution.py:33
  100.0 6.2 %collective-permute-done.1 = f32[128,128]{1,0:T(8,128)S(1)} collective-permute-done((f32[128,128]{1,0:T(8,128)S(1)}, f32[128,128]{1,0:T(8,128)S(1)}, u32[]{:S(2)}, u32[]{:S(2)}) %collective-permute-start.1) | collective-permute-done | bytes 65568 | tf_op jit(solution)/shard_map/ppermute | solution.py:33
  106.2 0.6 copy.25
  (7 shorter events, 0.1 us)
Async XLA Ops:
  0.0 8.0 %copy-start.1 = (s32[2,6]{1,0:T(2,128)S(1)}, s32[2,6]{1,0:T(2,128)}, u32[]{:S(2)}) copy-start(s32[2,6]{1,0:T(2,128)} %param.6) | copy-start | bytes 148
  0.0 8.2 %copy-start = (f32[128,384]{1,0:T(8,128)S(1)}, f32[128,384]{1,0:T(8,128)}, u32[]{:S(2)}) copy-start(f32[128,384]{1,0:T(8,128)} %param.4) | copy-start | bytes 589828
  2.1 30.7 %collective-permute-start = (f32[384,256]{0,1:T(8,128)S(1)}, f32[384,256]{0,1:T(8,128)S(1)}, u32[]{:S(2)}, u32[]{:S(2)}) collective-permute-start(f32[384,256]{0,1:T(8,128)S(1)} %bitcast_multiply_fusion), channel_id=1, source_target_pairs={{0,64},{64,0},{1,65},{65,1},{2,66},{66,2},{3,67},{67,3},{4,68},{68... | collective-permute-start | bytes 1179656 | tf_op jit(solution)/shard_map/ppermute | solution.py:15
  93.8 12.5 %collective-permute-start.1 = (f32[128,128]{1,0:T(8,128)S(1)}, f32[128,128]{1,0:T(8,128)S(1)}, u32[]{:S(2)}, u32[]{:S(2)}) collective-permute-start(f32[128,128]{1,0:T(8,128)S(1)} %reduce_sum.19), channel_id=1, source_target_pairs={{0,0},{8,128},{16,256},{24,384},{128,8},{136,136},{144,264},{152,3... | collective-permute-start | bytes 196616 | tf_op jit(solution)/shard_map/ppermute | solution.py:33
where the time goes:
time: 107 us
  blocking collectives  84.2 us (79%)
  starting transfers between devices  9.76 us (9%)
  waiting for transfers between devices  6.19 us (6%)
  matrix products  2.78 us (3%)
  local copies, waits for them, and re-layouts  2.71 us (3%)
  other arithmetic  1.09 us (1%)
    all_to_all x1, blocking collectives, body(): parts = lax.all_to_all(partial_sum, 'x', 0, 0, tiled=True)  28.5 us
    all_to_all x1, blocking collectives, body(): pieces = lax.all_to_all(pieces, 'z', 0, 0, tiled=True)  26.5 us
    all_gather x1, blocking collectives, body(): rows = lax.all_gather(masked_t, 'h', axis=0, tiled=True)  24.4 us
    ppermute x1, starting transfers between devices, body(): return lax.ppermute(total, ('h', 'x'), swap)  6.28 us
    ppermute x1, waiting for transfers between devices, body(): return lax.ppermute(total, ('h', 'x'), swap)  6.19 us
    ppermute x1, starting transfers between devices, body(): other_v = lax.ppermute(masked_v, 'l', [(0, 1), (1, 0)])  3.48 us
    dot_general x1, matrix products, body(): jnp.dot(rows, columns, precision=lax.Precision.HIGH, preferred_element_ty...  2.78 us
    all_gather x1, blocking collectives, body(): near = lax.all_gather(masked_v, 'c', axis=1, tiled=True)  2.37 us
  transfers between devices with their start and end apart: 2, of which 1 were waited for; matrix products, arithmetic and copies ran while one was open for 0% of the time, Pallas kernels for 0%

commit v1 on v0

--- a/solution.py
+++ b/solution.py
@@ -15,8 +15,11 @@
     other_v = lax.ppermute(masked_v, "l", [(0, 1), (1, 0)])
     masked_t = amplitudes * expand(pair_mask, tile_width)
     rows = lax.all_gather(masked_t, "h", axis=0, tiled=True)
-    near = lax.all_gather(masked_v, "c", axis=1, tiled=True)
-    far = lax.all_gather(other_v, "c", axis=1, tiled=True)
+    near, far = jnp.split(
+        lax.all_gather(jnp.concatenate([masked_v, other_v], axis=0), "c", axis=1, tiled=True),
+        [masked_v.shape[0]],
+        axis=0,
+    )
     low = lax.axis_index("l") == 0
     columns = jnp.concatenate([jnp.where(low, near, far), jnp.where(low, far, near)], axis=1)
     partial_sum = jnp.dot(

time: 107 us -> 125 us (1.17)
  the two profiles are of different devices: /device:TPU:4 before, /device:TPU:40 now
where the time goes in v1:
time: 125 us; the launch traced here: 124 us
  blocking collectives  72.9 us (58%)
  waiting for transfers between devices  23.8 us (19%)
  between operations  13.5 us (11%)
  starting transfers between devices  5.4 us (4%)
  other arithmetic  3.37 us (3%)
  matrix products  2.77 us (2%)
  local copies, waits for them, and re-layouts  2.72 us (2%)
    all_to_all x1, blocking collectives, body(): parts = lax.all_to_all(partial_sum, 'x', 0, 0, tiled=True)  30.8 us
    all_to_all x1, blocking collectives, body(): pieces = lax.all_to_all(pieces, 'z', 0, 0, tiled=True)  24 us
    all_gather x1, blocking collectives, body(): rows = lax.all_gather(masked_t, 'h', axis=0, tiled=True)  18 us
    ppermute x1, waiting for transfers between devices, body(): return lax.ppermute(total, ('h', 'x'), swap)  10.4 us
    ppermute x1, waiting for transfers between devices, body(): other_v = lax.ppermute(masked_v, 'l', [(0, 1), (1, 0)])  9.48 us
    all_gather x1, waiting for transfers between devices, body(): lax.all_gather(jnp.concatenate([masked_v, other_v], axis=0), 'c', axis=1,...  3.84 us
    ppermute x1, starting transfers between devices, body(): other_v = lax.ppermute(masked_v, 'l', [(0, 1), (1, 0)])  3.39 us
    dot_general x1, matrix products, body(): jnp.dot(rows, columns, precision=lax.Precision.HIGH, preferred_element_ty...  2.77 us
  transfers between devices with their start and end apart: 3, of which 3 were waited for; matrix products, arithmetic and copies ran while one was open for 0% of the time, Pallas kernels for 0%

profile of v1, /device:TPU:40, one launch (start us, length us, event | category | flops | bytes accessed | tf_op | source)
XLA Modules:
  0.0 124.4 jit_solution(16396492333823880271)
XLA Ops:
  6.5 0.7 convert_element_type.7
  7.2 0.1 broadcast_in_dim.14
  7.3 0.1 reshape.21
  7.4 1.2 copy.21
  8.6 3.4 %collective-permute-start = (f32[384,256]{0,1:T(8,128)S(1)}, f32[384,256]{0,1:T(8,128)S(1)}, u32[]{:S(2)}, u32[]{:S(2)}) collective-permute-start(f32[384,256]{0,1:T(8,128)S(1)} %bitcast_multiply_fusion), channel_id=1, source_target_pairs={{0,64},{64,0},{1,65},{65,1},{2,66},{66,2},{3,67},{67,3},{4,68},{68... | collective-permute-start | bytes 1179656 | tf_op jit(solution)/shard_map/ppermute | solution.py:15
  12.0 9.5 %collective-permute-done = f32[384,256]{0,1:T(8,128)S(1)} collective-permute-done((f32[384,256]{0,1:T(8,128)S(1)}, f32[384,256]{0,1:T(8,128)S(1)}, u32[]{:S(2)}, u32[]{:S(2)}) %collective-permute-start) | collective-permute-done | bytes 393248 | tf_op jit(solution)/shard_map/ppermute | solution.py:15
  21.5 0.9 pad_maximum_fusion
  22.4 0.0 all-gather.2.cloned.1.call-update
  22.5 0.1 copy.19
  22.6 0.1 broadcast_in_dim.12
  22.6 0.1 reshape.19
  22.7 0.1 copy.20
  22.9 18.0 %all_gather.6 = f32[512,384]{0,1:T(8,128)S(1)} all-gather(f32[128,384]{0,1:T(8,128)S(1)} %bitcast_multiply_fusion.1), channel_id=1, replica_groups=mesh['h'=4,'l'=2,'c'=2,'x'=4,'z'=8] {'h'}, dimensions={0}, use_global_device_ids=true | all-gather | bytes 983040 | tf_op jit(solution)/shard_map/all_gather | solution.py:17
  40.9 3.8 %all-gather.2.cloned.1.call-done = f32[768,512]{0,1:T(8,128)} async-done(((f32[768,256]{0,1:T(8,128)}), f32[768,512]{0,1:T(8,128)}) %all-gather.2.cloned.1.call-update) | async-done | bytes 1572880 | tf_op jit(solution)/shard_map/all_gather | solution.py:19
  44.7 1.5 %slice_select_fusion.1 = (f32[384,512]{0,1:T(8,128)S(1)}, f32[384,512]{0,1:T(8,128)S(1)}) fusion(f32[768,512]{0,1:T(8,128)} %all-gather.2.cloned.1.call-done, pred[]{:T(512)S(6)} %eq.3), kind=kLoop, calls=%fused_computation.6 | loop fusion | flops 393216 | bytes 3145729 | tf_op jit(solution)/shard_map/jit(_where)/select_n | solution.py:24
  46.2 2.8 %fusion = f32[512,1024]{1,0:T(8,128)S(1)} fusion(f32[512,384]{0,1:T(8,128)S(1)} %all_gather.6, f32[384,512]{0,1:T(8,128)S(1)} %get-tuple-element.6, f32[384,512]{0,1:T(8,128)S(1)} %get-tuple-element.5), kind=kOutput, calls=%fused_computation | convolution fusion | flops 1208352768 | bytes 4456448 | tf_op jit(solution)/shard_map/dot_general | solution.py:25
  49.0 30.8 %all_to_all.14 = f32[4,128,1024]{2,1,0:T(8,128)S(1)} all-to-all(f32[4,128,1024]{2,1,0:T(8,128)S(1)} %bitcast.13), channel_id=1, replica_groups=mesh['h'=4,'l'=2,'c'=2,'x'=4,'z'=8] {'x'}, dimensions={0} | all-to-all | bytes 4194304 | tf_op jit(solution)/shard_map/all_to_all | solution.py:29
  79.8 0.2 reduce_sum.18
  80.0 0.2 copy.22
  80.2 0.2 copy.23
  80.4 24.0 %all_to_all.15 = f32[8,128,128]{2,1,0:T(8,128)S(1)} all-to-all(f32[8,128,128]{2,1,0:T(8,128)S(1)} %copy.23), channel_id=1, replica_groups=mesh['h'=4,'l'=2,'c'=2,'x'=4,'z'=8] {'z'}, dimensions={0} | all-to-all | bytes 1048576 | tf_op jit(solution)/shard_map/all_to_all | solution.py:33
  104.5 2.0 %collective-permute-start.1 = (f32[128,128]{1,0:T(8,128)S(1)}, f32[128,128]{1,0:T(8,128)S(1)}, u32[]{:S(2)}, u32[]{:S(2)}) collective-permute-start(f32[128,128]{1,0:T(8,128)S(1)} %reduce_sum.19), channel_id=1, source_target_pairs={{0,0},{8,128},{16,256},{24,384},{128,8},{136,136},{144,264},{152,3... | collective-permute-start | bytes 196616 | tf_op jit(solution)/shard_map/ppermute | solution.py:36
  106.5 10.4 %collective-permute-done.1 = f32[128,128]{1,0:T(8,128)S(1)} collective-permute-done((f32[128,128]{1,0:T(8,128)S(1)}, f32[128,128]{1,0:T(8,128)S(1)}, u32[]{:S(2)}, u32[]{:S(2)}) %collective-permute-start.1) | collective-permute-done | bytes 65568 | tf_op jit(solution)/shard_map/ppermute | solution.py:36
  117.0 0.6 copy.25
  (9 shorter events, 0.1 us)
Async XLA Ops:
  6.5 38.2 %all-gather.2.cloned.1.call-start = ((), (), s32[]{:S(2)}) async-start(), calls=%async_computation.2 | async-start | bytes 2359296 | tf_op jit(solution)/shard_map/all_gather | solution.py:19
  8.5 13.9 %copy-start.1 = (s32[2,6]{1,0:T(2,128)S(1)}, s32[2,6]{1,0:T(2,128)}, u32[]{:S(2)}) copy-start(s32[2,6]{1,0:T(2,128)} %param.6) | copy-start | bytes 148
  8.6 14.2 %copy-start = (f32[128,384]{1,0:T(8,128)S(1)}, f32[128,384]{1,0:T(8,128)}, u32[]{:S(2)}) copy-start(f32[128,384]{1,0:T(8,128)} %param.4) | copy-start | bytes 589828
  8.6 12.9 %collective-permute-start = (f32[384,256]{0,1:T(8,128)S(1)}, f32[384,256]{0,1:T(8,128)S(1)}, u32[]{:S(2)}, u32[]{:S(2)}) collective-permute-start(f32[384,256]{0,1:T(8,128)S(1)} %bitcast_multiply_fusion), channel_id=1, source_target_pairs={{0,64},{64,0},{1,65},{65,1},{2,66},{66,2},{3,67},{67,3},{4,68},{68... | collective-permute-start | bytes 1179656 | tf_op jit(solution)/shard_map/ppermute | solution.py:15
  104.5 12.5 %collective-permute-start.1 = (f32[128,128]{1,0:T(8,128)S(1)}, f32[128,128]{1,0:T(8,128)S(1)}, u32[]{:S(2)}, u32[]{:S(2)}) collective-permute-start(f32[128,128]{1,0:T(8,128)S(1)} %reduce_sum.19), channel_id=1, source_target_pairs={{0,0},{8,128},{16,256},{24,384},{128,8},{136,136},{144,264},{152,3... | collective-permute-start | bytes 196616 | tf_op jit(solution)/shard_map/ppermute | solution.py:36
Sparse Core Ops, SparseCore 0:
  22.6 22.1 all-gather.1
